TPU v7x, 256 devices: a whole 4x4x8 slice. The times are simulated.
256 devices in a mesh: ctx: 32 (over x, z_lo, core), head: 8 (over y, z_hi).
Axes of the slice: x: 4, y: 4, z: 8 (z_hi: 2, z_lo: 4; z = z_hi * 4 + z_lo), core: 2. Of those that a mesh axis runs over, the one named last changes fastest.
Arguments:
- queries: bfloat16 [8192, 64, 128], P('ctx', 'head'), may hold values from -24 to 24, as said below
- self_keys: bfloat16 [8192, 8, 128], P('ctx', 'head'), may hold values from -24 to 24, as said below
- self_values: bfloat16 [8192, 8, 128], P('ctx', 'head'), may hold values from -6 to 6
- image_keys: bfloat16 [2048, 8, 128], P(('ctx', 'head')), may hold values from -24 to 24, as said below
- image_values: bfloat16 [2048, 8, 128], P(('ctx', 'head')), may hold values from -6 to 6
- image_offsets: int32 [4], replicated, may hold values from 0 to 8063, as said below
- first_image: int32 [64], replicated, may hold values from 0 to 4, as said below
- block_mask: int32 [64, 64], replicated, may hold values from 0 to 1, as said below
Outputs:
- self_attention: bfloat16 [8192, 64, 128], P('ctx', 'head')
- cross_attention: bfloat16 [8192, 64, 128], P('ctx', 'head')
Inputs may be any that keep to these rules, and one draw needn't show every extreme that they name: `queries`: within the stated range; both draws stay there. `self_keys`: within the stated range; both draws stay there. `image_keys`: within the stated range; both draws stay there. `image_offsets`: strictly increasing; the last image is inserted at 8063. first_image[b] is at most the number of images whose offset lies below (128 * (b + 1)); the last block's entry is 0 and the entry of block 62 is 4. block_mask[q, k] is 1 for k == q, 0 for k > q, and 0 or 1 below the diagonal.
All inputs are finite; a program needn't handle non-finite values.
Results may differ from a plain program's by a relative error of at most 0.0049.
Values may be sent and summed in bfloat16 or wider, within the bound.
A program may use at most 64 MiB of HBM per device.

v0:
```python
from functools import partial
import math

import jax
import jax.numpy as jnp
from jax import lax
from jax.sharding import PartitionSpec as P

IMG_LEN = 512
IMAGES = 4


masked_score = -1e30


def blend(carry_in, scores, allowed, value_rows, row_start, row_count):
    run_max, run_total, run_sum = carry_in
    old_max = run_max[:, :, row_start : row_start + row_count]
    old_total = run_total[:, :, row_start : row_start + row_count]
    old_sum = run_sum[:, :, row_start : row_start + row_count]
    scores = jnp.where(allowed, scores, masked_score)
    new_max = jnp.maximum(old_max, jnp.max(scores, axis=-1))
    weights = jnp.where(allowed, jnp.exp(scores - new_max[..., None]), 0.0)
    rescale = jnp.exp(old_max - new_max)
    new_total = old_total * rescale + jnp.sum(weights, axis=-1)
    added = jnp.einsum(
        "kgqs,skd->kgqd",
        weights.astype(jnp.bfloat16),
        value_rows,
        preferred_element_type=jnp.float32,
    )
    new_sum = old_sum * rescale[..., None] + added
    run_max = lax.dynamic_update_slice_in_dim(run_max, new_max, row_start, 2)
    run_total = lax.dynamic_update_slice_in_dim(run_total, new_total, row_start, 2)
    run_sum = lax.dynamic_update_slice_in_dim(run_sum, new_sum, row_start, 2)
    return (run_max, run_total, run_sum)


def keep_carry(carry_in):
    return carry_in


def per_device(
    queries,
    self_keys,
    self_values,
    image_keys,
    image_values,
    image_offsets,
    first_image,
    block_mask,
):
    tok_rows, heads_here, head_dim = queries.shape
    kv_here = self_keys.shape[1]
    group_size = heads_here // kv_here
    half_rows = tok_rows // 2
    ctx_index = lax.axis_index("ctx")
    root_dim = math.sqrt(head_dim)

    def block_of(device, which_half):
        return 2 * device + which_half

    grouped = queries.reshape(tok_rows, kv_here, group_size, head_dim)
    query_blocks = (block_of(ctx_index, 0), block_of(ctx_index, 1))
    row_ids = jnp.arange(half_rows, dtype=jnp.int32)
    diagonal = row_ids[:, None] >= row_ids[None, :]
    start_carry = (
        jnp.full((kv_here, group_size, tok_rows), masked_score, jnp.float32),
        jnp.zeros((kv_here, group_size, tok_rows), jnp.float32),
        jnp.zeros((kv_here, group_size, tok_rows, head_dim), jnp.float32),
    )

    def self_update(which_half, key_rows, value_rows, on_diagonal, carry_in):
        row_start = which_half * half_rows
        query_rows = grouped[row_start : row_start + half_rows]
        scores = (
            jnp.einsum("qkgd,skd->kgqs", query_rows, key_rows, preferred_element_type=jnp.float32)
            / root_dim
        )
        allowed = jnp.logical_or(jnp.logical_not(on_diagonal), diagonal)
        return blend(carry_in, scores, allowed[None, None], value_rows, row_start, half_rows)

    key_piece = lax.all_gather(self_keys, "ctx", axis=0, tiled=True)
    value_piece = lax.all_gather(self_values, "ctx", axis=0, tiled=True)
    steps_here = key_piece.shape[0] // half_rows

    def one_block(key_step, carry_in):
        key_rows = lax.dynamic_slice_in_dim(key_piece, key_step * half_rows, half_rows, 0)
        value_rows = lax.dynamic_slice_in_dim(value_piece, key_step * half_rows, half_rows, 0)
        key_block = block_of(key_step // 2, key_step % 2)
        for which_half in range(2):
            query_block = query_blocks[which_half]
            on_diagonal = key_block == query_block
            visible = on_diagonal | (key_block < query_block) & (
                block_mask[query_block, key_block] == 1
            )
            carry_in = lax.cond(
                visible,
                partial(self_update, which_half, key_rows, value_rows, on_diagonal),
                keep_carry,
                carry_in,
            )
        return carry_in

    self_state = lax.fori_loop(0, steps_here, one_block, start_carry)
    positions = jnp.concatenate(
        [query_blocks[0] * half_rows + row_ids, query_blocks[1] * half_rows + row_ids]
    )
    first_seen = jnp.concatenate(
        [
            jnp.full((half_rows,), first_image[query_blocks[0]], jnp.int32),
            jnp.full((half_rows,), first_image[query_blocks[1]], jnp.int32),
        ]
    )
    image_ids = jnp.arange(IMAGES, dtype=jnp.int32)
    head_start = lax.axis_index("head") * kv_here
    gathered = (
        lax.all_gather(image_keys, ("ctx", "head"), axis=0, tiled=True),
        lax.all_gather(image_values, ("ctx", "head"), axis=0, tiled=True),
    )
    key_rows = lax.dynamic_slice_in_dim(gathered[0], head_start, kv_here, 1)
    value_rows = lax.dynamic_slice_in_dim(gathered[1], head_start, kv_here, 1)
    row_count = key_rows.shape[0]
    image_index = jnp.arange(row_count, dtype=jnp.int32) // IMG_LEN
    row_offset = jnp.sum(
        jnp.where(image_index[:, None] == image_ids[None, :], image_offsets[None, :], 0), axis=1
    )
    allowed = (image_index[None, :] >= first_seen[:, None]) & (
        row_offset[None, :] <= positions[:, None]
    )
    scores = (
        jnp.einsum("qkgd,skd->kgqs", grouped, key_rows, preferred_element_type=jnp.float32)
        / root_dim
    )
    cross_state = blend(start_carry, scores, allowed[None, None], value_rows, 0, tok_rows)
    self_total = self_state[1]
    self_out = self_state[2] / self_total[..., None]
    self_out = (
        self_out.transpose(2, 0, 1, 3).reshape(tok_rows, heads_here, head_dim).astype(jnp.bfloat16)
    )
    cross_total = cross_state[1]
    has_image = cross_total > 0
    cross_out = jnp.where(
        has_image[..., None],
        cross_state[2] / jnp.where(has_image, cross_total, 1.0)[..., None],
        0.0,
    )
    cross_out = (
        cross_out.transpose(2, 0, 1, 3).reshape(tok_rows, heads_here, head_dim).astype(jnp.bfloat16)
    )
    return (self_out, cross_out)


def solution(mesh):
    return jax.shard_map(
        per_device,
        mesh=mesh,
        in_specs=(
            P("ctx", "head", None),
            P("ctx", "head", None),
            P("ctx", "head", None),
            P(("ctx", "head"), None, None),
            P(("ctx", "head"), None, None),
            P(),
            P(),
            P(),
        ),
        out_specs=(P("ctx", "head", None), P("ctx", "head", None)),
        check_vma=False,
    )
```

profile of v0, /device:TPU:7, one launch (start us, length us, event | category | flops | bytes accessed | tf_op | source)
XLA Modules:
  0.0 1242.2 jit_solution(8054559708324355680)
XLA Ops:
  15.9 1.4 compare_and_fusion
  17.4 55.1 %all-gather.5.cloned.1.call-done = bf16[8192,1,128]{2,0,1:T(8,128)(2,1)} async-done(((bf16[256,1,128]{2,0,1:T(8,128)(2,1)}), bf16[8192,1,128]{2,0,1:T(8,128)(2,1)}) %all-gather.5.cloned.1.call-update) | async-done | bytes 2097168 | tf_op jit(solution)/shard_map/all_gather | solution.py:83
  72.5 60.9 %all-gather.7.cloned.1.call-done = bf16[8192,1,128]{2,0,1:T(8,128)(2,1)} async-done(((bf16[256,1,128]{2,0,1:T(8,128)(2,1)}), bf16[8192,1,128]{2,0,1:T(8,128)(2,1)}) %all-gather.7.cloned.1.call-update) | async-done | bytes 2097168 | tf_op jit(solution)/shard_map/all_gather | solution.py:84
  133.5 278.2 %while.21 = (s32[]{:T(128)}, f32[1,8,256]{2,1,0:T(8,128)S(1)}, f32[1,8,256]{2,1,0:T(8,128)S(1)}, f32[1,8,256,128]{3,2,1,0:T(8,128)S(1)}, s32[]{:T(128)}, /*index...) while((s32[]{:T(128)}, f32[1,8,256]{2,1,0:T(8,128)S(1)}, ...), condition=%wide.region_9.10_spmd.clone.clone, body=%wide.region_0.9_spmd.clone.clone.sunk | while | flops 137156640 | bytes 6333146 | solution.py:105
  134.4 1.4 fusion.74
  138.8 1.4 fusion.74
  142.3 1.4 fusion.74
  146.7 1.4 fusion.74
  151.1 1.4 fusion.74
  155.5 1.4 fusion.74
  160.8 1.4 fusion.74
  165.2 1.4 fusion.74
  169.6 1.4 fusion.74
  174.0 1.4 fusion.74
  178.4 1.4 fusion.74
  192.5 1.4 fusion.74
  197.8 1.4 fusion.74
  206.6 1.4 fusion.74
  215.4 1.4 fusion.74
  223.3 1.4 fusion.74
  227.7 1.4 fusion.74
  240.9 1.4 fusion.74
  254.1 1.4 fusion.74
  259.3 1.4 fusion.74
  264.6 1.4 fusion.74
  279.5 1.4 fusion.74
  288.3 1.4 fusion.74
  301.5 1.4 fusion.74
  309.5 1.4 fusion.74
  313.9 1.4 fusion.74
  328.8 1.4 fusion.74
  337.6 1.4 fusion.74
  342.8 1.4 fusion.74
  351.7 1.4 fusion.74
  360.5 1.4 fusion.74
  365.7 1.4 fusion.74
  380.7 1.4 fusion.74
  387.8 1.4 fusion.74
  394.9 1.4 fusion.74
  405.5 1.4 fusion.74
  409.0 1.4 fusion.74
  411.9 1.5 fusion.59
  413.4 267.4 %all-gather.9.cloned.1.call-done = bf16[2048,8,128]{2,0,1:T(8,128)(2,1)} async-done(((bf16[8,8,128]{2,0,1:T(8,128)(2,1)}), bf16[2048,8,128]{2,0,1:T(8,128)(2,1)}) %all-gather.9.cloned.1.call-update) | async-done | bytes 4194320 | tf_op jit(solution)/shard_map/all_gather | solution.py:118
  680.8 3.7 fusion.38
  684.5 5.7 copy-done
  690.2 4.0 fusion.40
  694.2 531.7 %all-gather.11.cloned.1.call-done = bf16[2048,8,128]{2,0,1:T(8,128)(2,1)} async-done(((bf16[8,8,128]{2,0,1:T(8,128)(2,1)}), bf16[2048,8,128]{2,0,1:T(8,128)(2,1)}) %all-gather.11.cloned.1.call-update) | async-done | bytes 4194320 | tf_op jit(solution)/shard_map/all_gather | solution.py:119
  1225.9 8.6 fusion.51
  (672 shorter events, 200.8 us)
Async XLA Ops:
  7.2 65.3 %all-gather.5.cloned.1.call-start = ((), (), s32[]{:S(2)}) async-start(), calls=%async_computation | async-start | bytes 2162688 | tf_op jit(solution)/shard_map/all_gather | solution.py:83
  7.9 125.5 %all-gather.7.cloned.1.call-start = ((), (), s32[]{:S(2)}) async-start(), calls=%async_computation.1 | async-start | bytes 2162688 | tf_op jit(solution)/shard_map/all_gather | solution.py:84
  8.6 672.1 %all-gather.9.cloned.1.call-start = ((), (), s32[]{:S(2)}) async-start(), calls=%async_computation.2 | async-start | bytes 4210688 | tf_op jit(solution)/shard_map/all_gather | solution.py:118
  10.0 1215.9 %all-gather.11.cloned.1.call-start = ((), (), s32[]{:S(2)}) async-start(), calls=%async_computation.3 | async-start | bytes 4210688 | tf_op jit(solution)/shard_map/all_gather | solution.py:119
  133.5 547.3 %copy-start.1 = (bf16[256,8,128]{2,1,0:T(8,128)(2,1)S(1)}, bf16[256,8,128]{2,1,0:T(8,128)(2,1)}, u32[]{:S(2)}) copy-start(bf16[256,8,128]{2,1,0:T(8,128)(2,1)} %param.14) | copy-start | bytes 1572868
  684.4 5.7 copy-start
Sparse Core Ops, SparseCore 0:
  9.9 62.5 all-gather.4
  74.3 59.0 all-gather.6
  135.8 544.9 all-gather.8
  682.4 543.4 all-gather.10
where the time goes:
time: 1250 us; the launch traced here: 1240 us
  waiting for transfers between devices  917 us (73%)
  local copies, waits for them, and re-layouts  152 us (12%)
  loops' own time  90 us (7%)
  matrix products  52.8 us (4%)
  other arithmetic  17 us (1%)
  between operations  13.9 us (1%)
    all_gather x1, waiting for transfers between devices, per_device(): lax.all_gather(image_values, ('ctx', 'head'), axis=0, tiled=True)  532 us
    all_gather x1, waiting for transfers between devices, per_device(): lax.all_gather(image_keys, ('ctx', 'head'), axis=0, tiled=True)  267 us
    dynamic_slice x64, local copies, waits for them, and re-layouts, one_block(): block_mask[query_block, key_block] == 1  88.1 us
    another operation x1, loops' own time, per_device(): self_state = lax.fori_loop(0, steps_here, one_block, start_carry)  85.3 us
    all_gather x1, waiting for transfers between devices, per_device(): value_piece = lax.all_gather(self_values, 'ctx', axis=0, tiled=True)  60.9 us
    all_gather x1, waiting for transfers between devices, per_device(): key_piece = lax.all_gather(self_keys, 'ctx', axis=0, tiled=True)  55.1 us
    dynamic_slice x64, local copies, waits for them, and re-layouts, one_block(): lax.dynamic_slice_in_dim(value_piece, key_step * half_rows, half_rows, 0)  50.3 us
    dot_general x61, matrix products, blend(): jnp.einsum('kgqs,skd->kgqd', weights.astype(jnp.bfloat16), value_rows, pr...  34.7 us
  transfers between devices with their start and end apart: 4, of which 4 were waited for; matrix products, arithmetic and copies ran while one was open for 17% of the time, Pallas kernels for 0%

commit v1 on v0

v1 whole, which is shorter than its diff:
```python
import functools
import math

import jax
import jax.numpy as jnp
from jax import lax
from jax.experimental import pallas as pl
from jax.experimental.pallas import tpu as pltpu
from jax.sharding import PartitionSpec as P

MESH = pl.DeviceIdType.MESH
BF16 = jnp.bfloat16
F32 = jnp.float32

HEADS = 8
XS, ZS = 4, 4
BLK = 128
GROUP = 8
ROWS = BLK * GROUP
IMAGES = 4
IMG_LEN = 512
TILE = 128
SPAN = 8
LOG2E = 1.4426950408889634
HIDDEN = -1e30
FLOOR = -1e28


def gather_kernel(
    k_ref, v_ref, ik_ref, iv_ref, kv, img,
    own, own_img, outbox, inbox,
    piece_s, piece_r, zs, zr, xs, xr, rs, rr, sibs, sibr, ixs, ixr, izs, izr, isibs, isibr, keep,
):
    c = lax.axis_index("ctx")
    h = lax.axis_index("head")
    x, z, a = c // 8, (c // 2) % 4, c % 2
    left, right, far = (x + 3) % 4, (x + 1) % 4, (x + 2) % 4
    order = (z, z + 1 - 2 * (z % 2), 2 - z // 2, 3 - 3 * (z // 2))
    inner = z * (3 - z) > 0
    near, beyond = 3 - z, 3 * (z - 1)

    def ctx(x_, z_, a_):
        return x_ * 8 + z_ * 2 + a_

    def ks(x_, z_, a_):
        return a_ * 16 + x_ * 4 + z_

    def si(x_, z_, a_):
        return a_ * 16 + z_ * 4 + x_

    def rcopy(src, dst, ssem, rsem, to_ctx, to_head):
        return pltpu.make_async_remote_copy(
            src_ref=src, dst_ref=dst, send_sem=ssem, recv_sem=rsem,
            device_id=(to_ctx, to_head), device_id_type=MESH,
        )

    pending = []

    def send(src, dst, ssem, rsem, to_ctx, to_head, when=None):
        def go():
            rcopy(src, dst, ssem, rsem, to_ctx, to_head).start()

        def done():
            rcopy(src, dst, ssem, rsem, to_ctx, to_head).wait_send()

        if when is None:
            go()
        else:
            pl.when(when)(go)
        pending.append((when, done))

    def arrived(dst, rsem):
        rcopy(dst, dst, rsem, rsem, ctx(x, z, 1 - a), h).wait_recv()

    barrier = pltpu.get_barrier_semaphore()

    def greet(to_ctx, to_head):
        pl.semaphore_signal(barrier, inc=1, device_id=(to_ctx, to_head), device_id_type=MESH)

    greet(ctx(x, z, 1 - a), h)
    for x_ in (left, right, far):
        greet(ctx(x_, z, a), h)
    for d in range(1, HEADS):
        greet(c, (h + d) % HEADS)

    @pl.when(z > 0)
    def _():
        greet(ctx(x, z - 1, a), h)

    @pl.when(z < 3)
    def _():
        greet(ctx(x, z + 1, a), h)

    both = jnp.concatenate([ik_ref[...].astype(F32), iv_ref[...].astype(F32)], axis=0)
    outbox[...] = jnp.swapaxes(both, 0, 1).astype(BF16)
    own[:256] = k_ref[...]
    own[256:] = v_ref[...]
    keep_own = pltpu.make_async_copy(own, kv.at[ks(x, z, a)], keep.at[0])
    keep_own.start()

    pl.semaphore_wait(barrier, 12 + (z + 3) // 4 - z // 3)

    for d in range(1, HEADS):
        to = (h + d) % HEADS
        send(outbox.at[to], inbox.at[d], piece_s.at[d], piece_r.at[d], c, to)

    def own_column(i):
        s = ks(x, order[i], a)
        src = own if i == 0 else kv.at[s]
        send(src, kv.at[s], xs.at[0, i], xr.at[0, i], ctx(right, z, a), h)
        send(src, kv.at[s], xs.at[1, i], xr.at[1, i], ctx(left, z, a), h)
        share(0, i)

    def share(kind, i):
        s = ks((x, left, right, far)[kind], order[i], a)
        src = own if (kind, i) == (0, 0) else kv.at[s]
        send(src, kv.at[s], sibs.at[kind, i], sibr.at[kind, i], ctx(x, z, 1 - a), h)

    def column(i):
        s = ks(x, order[i], a)
        arrived(kv.at[s], zr.at[order[i]])
        to = near if i == 1 else beyond
        send(kv.at[s], kv.at[s], zs.at[i + 1], zr.at[order[i]], ctx(x, to, a), h, inner)
        own_column(i)

    def from_left(i):
        s = ks(left, order[i], a)
        arrived(kv.at[s], xr.at[0, i])
        if i < 2:
            send(kv.at[s], kv.at[s], rs.at[i], rr.at[i], ctx(right, z, a), h)
        share(1, i)

    def from_right(i):
        s = ks(right, order[i], a)
        arrived(kv.at[s], xr.at[1, i])
        if i >= 2:
            send(kv.at[s], kv.at[s], rs.at[i], rr.at[i], ctx(left, z, a), h)
        share(2, i)

    def from_far(i):
        s = ks(far, order[i], a)
        arrived(kv.at[s], rr.at[i])
        share(3, i)

    def image_line(i):
        part = img.at[pl.ds(si(0, order[i], a), 4)]
        send(part, part, isibs.at[i], isibr.at[i], ctx(x, z, 1 - a), h)
        return part

    def image_arrived(i):
        part = img.at[pl.ds(si(0, order[i], a), 4)]
        arrived(part, izr.at[order[i]])
        to = near if i == 1 else beyond
        send(part, part, izs.at[i + 1], izr.at[order[i]], ctx(x, to, a), h, inner)
        image_line(i)

    s = ks(x, z, a)
    send(own, kv.at[s], zs.at[0], zr.at[z], ctx(x, z + 1, a), h, z < 3)
    send(own, kv.at[s], zs.at[1], zr.at[z], ctx(x, z - 1, a), h, z > 0)
    own_column(0)

    inbox[0] = outbox[h]
    for d in range(1, HEADS):
        arrived(inbox.at[d], piece_r.at[d])
    rows = inbox[...].astype(F32)
    si_mine = si(x, z, a)
    own_img[:64] = rows[:, :8, :].reshape(64, 128).astype(BF16)
    own_img[64:] = rows[:, 8:, :].reshape(64, 128).astype(BF16)
    keep_img = pltpu.make_async_copy(own_img, img.at[si_mine], keep.at[1])
    keep_img.start()
    for d, x_ in ((1, right), (2, far), (3, left)):
        send(own_img, img.at[si_mine], ixs.at[d], ixr.at[d], ctx(x_, z, a), h)

    column(1)
    from_left(0)
    from_right(0)
    for d, x_ in ((1, left), (2, far), (3, right)):
        arrived(img.at[si(x_, z, a)], ixr.at[d])
    keep_img.wait()
    part = image_line(0)
    send(part, part, izs.at[0], izr.at[z], ctx(x, z + 1, a), h, z < 3)
    send(part, part, izs.at[1], izr.at[z], ctx(x, z - 1, a), h, z > 0)
    column(2)
    from_left(1)
    from_right(1)
    column(3)
    image_arrived(1)
    from_far(0)
    from_right(2)
    from_left(2)
    image_arrived(2)
    from_right(3)
    from_far(1)
    image_arrived(3)
    from_far(2)
    from_left(3)
    from_far(3)

    for kind in range(4):
        for i in range(4):
            s = ks((x, left, right, far)[kind], order[i], 1 - a)
            arrived(kv.at[s], sibr.at[kind, i])
    for i in range(4):
        first = si(0, order[i], 1 - a)
        arrived(img.at[pl.ds(first, 4)], isibr.at[i])
    keep_own.wait()
    for when, done in pending:
        if when is None:
            done()
        else:
            pl.when(when)(done)


def attend_kernel(
    offsets_ref, first_ref, mask_ref, q_ref, kv_ref, img_ref, self_ref, cross_ref,
    keys, vals, acc, top, bias, seen,
):
    c = lax.axis_index("ctx")
    scale = LOG2E / math.sqrt(128.0)
    vals[:, 128:] = jnp.ones((SPAN * BLK, 128), BF16)

    def reset():
        top[...] = jnp.full_like(top, FLOOR)
        acc[...] = jnp.zeros_like(acc)

    def step(i, extra):
        for r in range(ROWS // TILE):
            here = pl.ds(r * TILE, TILE)
            q = q_ref[pl.ds(i * ROWS + r * TILE, TILE), :]
            scores = lax.dot_general(
                q, keys[...], (((1,), (1,)), ((), ())), preferred_element_type=F32
            )
            scores = scores + extra(r)
            old = top[here, :]
            new = jnp.maximum(old, jnp.max(scores, axis=1, keepdims=True))
            top[here, :] = new
            weights = jnp.exp2((scores - new[:, :1]) * scale).astype(BF16)
            shrink = jnp.exp2((old - new) * scale)
            shrink = jnp.concatenate([shrink, shrink], axis=1)
            acc[here, :] = acc[here, :] * shrink + jnp.dot(
                weights, vals[...], preferred_element_type=F32
            )

    def result():
        total = acc[:, 128:]
        good = total > 0.0
        return jnp.where(good, acc[:, :128] / jnp.where(good, total, 1.0), 0.0).astype(BF16)

    def place(b):
        dev = b // 2
        return (dev % 2) * 16 + (dev // 8) * 4 + (dev // 2) % 4, (b % 2) * BLK

    for i in range(2):
        qb = 2 * c + i
        seen[0] = qb

        def collect(b, n):
            vis = mask_ref[qb, b]
            seen[n] = b
            return n + vis

        count = lax.fori_loop(0, qb, collect, jnp.int32(1))
        reset()

        def load(t, b):
            s, half = place(b)
            half = pl.multiple_of(half, BLK)
            keys[t * BLK:(t + 1) * BLK, :] = kv_ref[s, pl.ds(half, BLK), :]
            vals[t * BLK:(t + 1) * BLK, :128] = kv_ref[s, pl.ds(256 + half, BLK), :]

        def span(j, _):
            for t in range(SPAN):
                n = j * SPAN + t
                live = n < count
                load(t, jnp.where(live, seen[jnp.where(live, n, 0)], qb))
                bias[:, t * BLK:(t + 1) * BLK] = jnp.full(
                    (1, BLK), jnp.where(live, 0.0, HIDDEN), F32
                )

            @pl.when(j == 0)
            def _():
                def extra(r):
                    per = TILE // GROUP
                    at = lax.broadcasted_iota(jnp.int32, (TILE, BLK), 0) // GROUP + r * per
                    key = lax.broadcasted_iota(jnp.int32, (TILE, BLK), 1)
                    tri = jnp.where(key <= at, 0.0, HIDDEN)
                    rest = jnp.broadcast_to(bias[:, BLK:], (TILE, (SPAN - 1) * BLK))
                    return jnp.concatenate([tri, rest], axis=1)

                step(i, extra)

            @pl.when(j > 0)
            def _():
                step(i, lambda r: bias[...])

            return 0

        lax.fori_loop(0, (count + SPAN - 1) // SPAN, span, 0)
        self_ref[i * ROWS:(i + 1) * ROWS, :] = result()

        reset()
        for pair in range(IMAGES // 2):
            m0 = 2 * pair
            last = qb * BLK + BLK - 1

            def vis(m):
                return (m >= first_ref[qb]) & (offsets_ref[m] <= last)

            @pl.when(vis(m0) | vis(m0 + 1))
            def _():
                for m in (m0, m0 + 1):
                    for d in range(8):
                        s = (d % 2) * 16 + (d // 2) * 4 + m
                        row = (m - m0) * IMG_LEN + d * 64
                        keys[row:row + 64, :] = img_ref[s, :64, :]
                        vals[row:row + 64, :128] = img_ref[s, 64:, :]

                def extra(r):
                    per = TILE // GROUP
                    at = (
                        lax.broadcasted_iota(jnp.int32, (TILE, IMG_LEN), 0) // GROUP
                        + (r * per + qb * BLK)
                    )
                    parts = []
                    for m in (m0, m0 + 1):
                        lowest = jnp.where(m >= first_ref[qb], offsets_ref[m], 1 << 30)
                        parts.append(jnp.where(at >= lowest, 0.0, HIDDEN))
                    return jnp.concatenate(parts, axis=1)

                step(i, extra)

        cross_ref[i * ROWS:(i + 1) * ROWS, :] = result()


def per_device(q, k, v, ik, iv, offsets, first, mask):
    vmem = pl.BlockSpec(memory_space=pltpu.VMEM)
    smem = pl.BlockSpec(memory_space=pltpu.SMEM)
    hbm = pl.BlockSpec(memory_space=pl.ANY)
    dma = pltpu.SemaphoreType.DMA
    kv, img = pl.pallas_call(
        gather_kernel,
        out_shape=(
            jax.ShapeDtypeStruct((32, 512, 128), BF16),
            jax.ShapeDtypeStruct((32, 128, 128), BF16),
        ),
        in_specs=[vmem] * 4,
        out_specs=(hbm, hbm),
        scratch_shapes=[
            pltpu.VMEM((512, 128), BF16),
            pltpu.VMEM((128, 128), BF16),
            pltpu.VMEM((8, 16, 128), BF16),
            pltpu.VMEM((8, 16, 128), BF16),
            dma((8,)), dma((8,)),
            dma((5,)), dma((4,)),
            dma((2, 4)), dma((2, 4)),
            dma((4,)), dma((4,)),
            dma((4, 4)), dma((4, 4)),
            dma((4,)), dma((4,)),
            dma((5,)), dma((4,)),
            dma((4,)), dma((4,)),
            dma((2,)),
        ],
        compiler_params=pltpu.CompilerParams(
            collective_id=0, has_side_effects=True, vmem_limit_bytes=24 * 2**20
        ),
    )(k.reshape(-1, 128), v.reshape(-1, 128), ik, iv)

    n = q.shape[0] * q.shape[1]
    self_out, cross_out = pl.pallas_call(
        attend_kernel,
        out_shape=(jax.ShapeDtypeStruct((n, 128), BF16),) * 2,
        in_specs=[smem] * 3 + [vmem] * 3,
        out_specs=(vmem, vmem),
        scratch_shapes=[
            pltpu.VMEM((SPAN * BLK, 128), BF16),
            pltpu.VMEM((SPAN * BLK, 256), BF16),
            pltpu.VMEM((ROWS, 256), F32),
            pltpu.VMEM((ROWS, 128), F32),
            pltpu.VMEM((1, SPAN * BLK), F32),
            pltpu.SMEM((128,), jnp.int32),
        ],
        compiler_params=pltpu.CompilerParams(vmem_limit_bytes=40 * 2**20),
    )(offsets, first, mask, q.reshape(n, 128), kv, img)
    return self_out.reshape(q.shape), cross_out.reshape(q.shape)


def solution(mesh):
    return jax.shard_map(
        per_device,
        mesh=mesh,
        in_specs=(
            P("ctx", "head", None),
            P("ctx", "head", None),
            P("ctx", "head", None),
            P(("ctx", "head"), None, None),
            P(("ctx", "head"), None, None),
            P(),
            P(),
            P(),
        ),
        out_specs=(P("ctx", "head", None), P("ctx", "head", None)),
        check_vma=False,
    )
```

time: 1250 us -> 71.7 us (0.06)
  waiting for transfers between devices: 917 us -> 0 us
  local copies, waits for them, and re-layouts: 152 us -> 6.21 us
  loops' own time: 90 us -> 0 us
  Pallas kernels: 0 us -> 64.4 us
  matrix products: 52.8 us -> 0 us
  other arithmetic: 17 us -> 0 us
  between operations: 13.9 us -> 0.66 us
    all_gather x4 -> x0, waiting for transfers between devices: 915 us -> none  [the longest x1 532 us: per_device(): lax.all_gather(image_values, ('ctx', 'head'), axis=0, tiled=True)]
    dynamic_slice x129 -> x0, local copies, waits for them, and re-layouts: 140 us -> none  [the longest x64 88.1 us: one_block(): block_mask[query_block, key_block] == 1]
    another operation x129 -> x0, loops' own time: 90 us -> none  [the longest x1 85.3 us: per_device(): self_state = lax.fori_loop(0, steps_here, one_block, start_carry)]
    pallas_call x0 -> x2, Pallas kernels: none -> 64.4 us  [the longest x1 38.7 us: per_device(): pl.pallas_call(gather_kernel, out_shape=(jax.ShapeDtypeStruct((32, 512, 1...]
    dot_general x122 -> x0, matrix products: 52.8 us -> none  [the longest x61 34.7 us: blend(): jnp.einsum('kgqs,skd->kgqd', weights.astype(jnp.bfloat16), value_rows, pr...]
  transfers between devices with their start and end apart: 4 -> 0, of which waited for: 4 -> 0; matrix products, arithmetic and copies ran while one was open for 17% -> 0% of each run, Pallas kernels for 0% -> 0%
where the time goes in v1:
time: 71.7 us; the launch traced here: 71.2 us
  Pallas kernels  64.4 us (90%)
  local copies, waits for them, and re-layouts  6.21 us (9%)
    pallas_call x1, Pallas kernels, per_device(): pl.pallas_call(gather_kernel, out_shape=(jax.ShapeDtypeStruct((32, 512, 1...  38.7 us
    pallas_call x1, Pallas kernels, per_device(): pl.pallas_call(attend_kernel, out_shape=(jax.ShapeDtypeStruct((n, 128), B...  25.7 us
    unnamed x16, local copies, waits for them, and re-layouts  6.21 us

profile of v1, /device:TPU:7, one launch (start us, length us, event | category | flops | bytes accessed | tf_op | source)
XLA Modules:
  0.0 71.2 jit_solution(10544916739059677886)
XLA Ops:
  0.6 0.0 copy-start.1
  0.6 0.8 %copy-done.1 = bf16[256,1,128]{2,0,1:T(8,128)(2,1)S(1)} copy-done((bf16[256,1,128]{2,0,1:T(8,128)(2,1)S(1)}, bf16[256,1,128]{2,0,1:T(8,128)(2,1)}, u32[]{:S(2)}) %copy-start.1) | copy-done | bytes 65560
  1.5 0.0 copy-start.2
  1.5 0.8 %copy-done.2 = bf16[256,1,128]{2,0,1:T(8,128)(2,1)S(1)} copy-done((bf16[256,1,128]{2,0,1:T(8,128)(2,1)S(1)}, bf16[256,1,128]{2,0,1:T(8,128)(2,1)}, u32[]{:S(2)}) %copy-start.2) | copy-done | bytes 65560
  2.3 0.0 copy-start.4
  2.3 0.7 %copy-done.4 = bf16[8,8,128]{2,1,0:T(8,128)(2,1)S(1)} copy-done((bf16[8,8,128]{2,1,0:T(8,128)(2,1)S(1)}, bf16[8,8,128]{2,1,0:T(8,128)(2,1)}, u32[]{:S(2)}) %copy-start.4) | copy-done | bytes 16408
  3.0 0.0 copy-start.5
  3.0 0.7 %copy-done.5 = bf16[8,8,128]{2,1,0:T(8,128)(2,1)S(1)} copy-done((bf16[8,8,128]{2,1,0:T(8,128)(2,1)S(1)}, bf16[8,8,128]{2,1,0:T(8,128)(2,1)}, u32[]{:S(2)}) %copy-start.5) | copy-done | bytes 16408
  3.7 38.7 %shard_map.95 = (bf16[32,512,128]{2,1,0:T(8,128)(2,1)S(1)}, bf16[32,128,128]{2,1,0:T(8,128)(2,1)S(1)}) custom-call(bf16[256,128]{1,0:T(8,128)(2,1)S(1)} %bitcast.6, bf16[256,128]{1,0:T(8,128)(2,1)S(1)} %bitcast.7, bf16[8,8,128]{2,1,0:T(8,128)(2,1)S(1)} %copy-done.4, bf16[8,8,128]{2,1,0:T(8,128)(2,1)S(1)} %copy-done.5), custom_call_target="tpu_custom_call" | custom-call | tf_op jit(solution)/shard_map/pallas_call | solution.py:340
  42.4 0.0 copy-start
  42.4 1.0 %copy-done = bf16[256,8,128]{2,1,0:T(8,128)(2,1)S(1)} copy-done((bf16[256,8,128]{2,1,0:T(8,128)(2,1)S(1)}, bf16[256,8,128]{2,1,0:T(8,128)(2,1)}, u32[]{:S(2)}) %copy-start) | copy-done | bytes 524312
  43.5 0.0 copy-start.3
  43.5 0.8 %copy-done.3 = s32[64,64]{1,0:T(8,128)S(1)} copy-done((s32[64,64]{1,0:T(8,128)S(1)}, s32[64,64]{1,0:T(8,128)}, u32[]{:S(2)}) %copy-start.3) | copy-done | bytes 16408
  44.2 0.0 copy-start.6
  44.2 0.7 copy-done.6
  44.9 0.0 copy-start.7
  44.9 0.7 copy-done.7
  45.5 25.7 %shard_map.96 = (bf16[2048,128]{1,0:T(8,128)(2,1)}, bf16[2048,128]{1,0:T(8,128)(2,1)}) custom-call(s32[4]{0:T(128)S(1)} %copy-done.6, s32[64]{0:T(128)S(1)} %copy-done.7, s32[64,64]{1,0:T(8,128)S(1)} %copy-done.3, bf16[2048,128]{1,0:T(8,128)(2,1)S(1)} %bitcast.5, bf16[32,512,128]{2,1,0:T(8,128)(2,1)S(1)} %get-tuple-element.6.kv_ref, ...), custom_call_target="tpu_custom_call" | custom-call | tf_op jit(solution)/shard_map/pallas_call | solution.py:369
Async XLA Ops:
  0.6 0.8 %copy-start.1 = (bf16[256,1,128]{2,0,1:T(8,128)(2,1)S(1)}, bf16[256,1,128]{2,0,1:T(8,128)(2,1)}, u32[]{:S(2)}) copy-start(bf16[256,1,128]{2,0,1:T(8,128)(2,1)} %param.9) | copy-start | bytes 196612
  1.5 0.8 %copy-start.2 = (bf16[256,1,128]{2,0,1:T(8,128)(2,1)S(1)}, bf16[256,1,128]{2,0,1:T(8,128)(2,1)}, u32[]{:S(2)}) copy-start(bf16[256,1,128]{2,0,1:T(8,128)(2,1)} %param.10) | copy-start | bytes 196612
  2.3 0.7 %copy-start.4 = (bf16[8,8,128]{2,1,0:T(8,128)(2,1)S(1)}, bf16[8,8,128]{2,1,0:T(8,128)(2,1)}, u32[]{:S(2)}) copy-start(bf16[8,8,128]{2,1,0:T(8,128)(2,1)} %ik_ref.1) | copy-start | bytes 49156
  3.0 0.7 %copy-start.5 = (bf16[8,8,128]{2,1,0:T(8,128)(2,1)S(1)}, bf16[8,8,128]{2,1,0:T(8,128)(2,1)}, u32[]{:S(2)}) copy-start(bf16[8,8,128]{2,1,0:T(8,128)(2,1)} %iv_ref.1) | copy-start | bytes 49156
  42.4 1.0 %copy-start = (bf16[256,8,128]{2,1,0:T(8,128)(2,1)S(1)}, bf16[256,8,128]{2,1,0:T(8,128)(2,1)}, u32[]{:S(2)}) copy-start(bf16[256,8,128]{2,1,0:T(8,128)(2,1)} %param.8) | copy-start | bytes 1572868
  43.5 0.8 %copy-start.3 = (s32[64,64]{1,0:T(8,128)S(1)}, s32[64,64]{1,0:T(8,128)}, u32[]{:S(2)}) copy-start(s32[64,64]{1,0:T(8,128)} %mask_ref.1) | copy-start | bytes 49156
  44.2 0.7 copy-start.6
  44.9 0.7 copy-start.7

commit v2 on v1

v2 whole, which is shorter than its diff:
```python
import functools
import math

import jax
import jax.numpy as jnp
from jax import lax
from jax.experimental import pallas as pl
from jax.experimental.pallas import tpu as pltpu
from jax.sharding import PartitionSpec as P

MESH = pl.DeviceIdType.MESH
BF16 = jnp.bfloat16
F32 = jnp.float32

HEADS = 8
XS, ZS = 4, 4
BLK = 128
GROUP = 8
ROWS = BLK * GROUP
IMAGES = 4
IMG_LEN = 512
TILE = 128
SPAN = 8
LATER = ((2, 1), (3, 1))
LAST = 31
LOG2E = 1.4426950408889634
HIDDEN = -1e30
FLOOR = -1e28


def soft_step(q_ref, keys, vals, acc, top, first_row, extra):
    scale = LOG2E / math.sqrt(128.0)
    for r in range(ROWS // TILE):
        here = pl.ds(first_row + r * TILE, TILE)
        scores = lax.dot_general(
            q_ref[here, :], keys[...], (((1,), (1,)), ((), ())), preferred_element_type=F32
        )
        scores = scores + extra(r)
        old = top[here, :]
        new = jnp.maximum(old, jnp.max(scores, axis=1, keepdims=True))
        top[here, :] = new
        weights = jnp.exp2((scores - new[:, :1]) * scale).astype(BF16)
        shrink = jnp.exp2((old - new) * scale)
        shrink = jnp.concatenate([shrink, shrink], axis=1)
        acc[here, :] = acc[here, :] * shrink + jnp.dot(
            weights, vals[...], preferred_element_type=F32
        )


def gather_kernel(
    k_hbm, v_hbm, ik_hbm, iv_hbm, q_hbm, mask_hbm, kv, img, acc, top,
    own, own_img, outbox, inbox, ik, iv, q, mask, keys, vals, bias,
    piece_s, piece_r, zs, zr, xs, xr, rs, rr, sibs, sibr, ixs, ixr, izs, izr, isibs, isibr, last_s, last_r, keep,
):
    c = lax.axis_index("ctx")
    h = lax.axis_index("head")
    x, z, a = c // 8, (c // 2) % 4, c % 2
    left, right, far = (x + 3) % 4, (x + 1) % 4, (x + 2) % 4
    order = (z, z + 1 - 2 * (z % 2), 2 - z // 2, 3 - 3 * (z // 2))
    final = (c // 24) * (31 - c) > 0

    def ctx(x_, z_, a_):
        return x_ * 8 + z_ * 2 + a_

    def ks(x_, z_, a_):
        return a_ * 16 + x_ * 4 + z_

    def si(x_, z_, a_):
        return a_ * 16 + z_ * 4 + x_

    def rcopy(src, dst, ssem, rsem, to_ctx, to_head):
        return pltpu.make_async_remote_copy(
            src_ref=src, dst_ref=dst, send_sem=ssem, recv_sem=rsem,
            device_id=(to_ctx, to_head), device_id_type=MESH,
        )

    pending = []

    def run(when, go):
        if when is None:
            go()
        else:
            pl.when(when)(go)

    def send(src, dst, ssem, rsem, to_ctx, to_head, when=None):
        run(when, lambda: rcopy(src, dst, ssem, rsem, to_ctx, to_head).start())
        pending.append(
            (when, lambda: rcopy(src, dst, ssem, rsem, to_ctx, to_head).wait_send())
        )

    def arrived(dst, rsem, when=None):
        run(when, lambda: rcopy(dst, dst, rsem, rsem, ctx(x, z, 1 - a), h).wait_recv())

    loads = [
        pltpu.make_async_copy(src, dst, keep.at[2 + n])
        for n, (src, dst) in enumerate((
            (k_hbm, own.at[pl.ds(0, 256)]), (v_hbm, own.at[pl.ds(256, 256)]),
            (ik_hbm, ik), (iv_hbm, iv), (q_hbm, q), (mask_hbm, mask),
        ))
    ]
    for load in loads:
        load.start()

    barrier = pltpu.get_barrier_semaphore()

    def greet(to_ctx, to_head):
        pl.semaphore_signal(barrier, inc=1, device_id=(to_ctx, to_head), device_id_type=MESH)

    for d in range(1, HEADS):
        greet(c, (h + d) % HEADS)
    greet(ctx(x, z, 1 - a), h)
    for x_ in (left, right, far):
        greet(ctx(x_, z, a), h)
    for dz in range(1, 4):
        greet(ctx(x, (z + dz) % 4, a), h)
    apart = (c // 24) * (1 - c // 29) * (1 - a)
    pl.when(apart > 0)(lambda: greet(LAST, h))

    @pl.when(c == LAST)
    def _():
        for n in (24, 26, 28):
            greet(n, h)

    loads[2].wait()
    loads[3].wait()
    both = jnp.concatenate([ik[...].astype(F32), iv[...].astype(F32)], axis=0)
    outbox[...] = jnp.swapaxes(both, 0, 1).astype(BF16)
    loads[0].wait()
    loads[1].wait()
    keep_own = pltpu.make_async_copy(own, kv.at[ks(x, z, a)], keep.at[0])
    keep_own.start()

    pl.semaphore_wait(barrier, 14 + apart + 3 * (c // LAST))

    for d in range(1, HEADS):
        to = (h + d) % HEADS
        send(outbox.at[to], inbox.at[d], piece_s.at[d], piece_r.at[d], c, to)

    def halves(ref):
        return ref.at[pl.ds(0, 256)], ref.at[pl.ds(256, 256)]

    def along_x(i, n):
        dst = halves(kv.at[ks(x, order[i], a)])[n]
        src = halves(own)[n] if i == 0 else dst
        send(src, dst, xs.at[n, 0, i], xr.at[n, 0, i], ctx(right, z, a), h, x < 3)
        send(src, dst, xs.at[n, 1, i], xr.at[n, 1, i], ctx(left, z, a), h, x == 0 if i < 2 else x < 2)

    def share(kind, i, when=None):
        s = ks((x, left, right, far)[kind], order[i], a)
        src = own if (kind, i) == (0, 0) else kv.at[s]
        send(src, kv.at[s], sibs.at[kind, i], sibr.at[kind, i], ctx(x, z, 1 - a), h, when)

    def column(i):
        s = ks(x, order[i], a)
        arrived(kv.at[s], zr.at[order[i]])
        along_x(i, 0)
        along_x(i, 1)
        share(0, i)

    def from_left(i):
        for n, part in enumerate(halves(kv.at[ks(left, order[i], a)])):
            arrived(part, xr.at[n, 0, i], x > 0)
            if i < 2:
                send(part, part, rs.at[n, i], rr.at[n, i], ctx(right, z, a), h, x * (3 - x) > 0)
        share(1, i, x > 0)

    def from_right(i):
        for n, part in enumerate(halves(kv.at[ks(right, order[i], a)])):
            arrived(part, xr.at[n, 1, i], x == 3 if i < 2 else x * (3 - x) == 0)
            if i >= 2:
                send(part, part, rs.at[n, i], rr.at[n, i], ctx(left, z, a), h, x * (3 - x) == 0)
        share(2, i, x == 3)

    def from_far(i):
        for n, part in enumerate(halves(kv.at[ks(far, order[i], a)])):
            arrived(part, rr.at[n, i], x > 1)
        share(3, i, x > 1)

    conds = (None, x > 0, x == 3, x > 1)

    def other_core(kind, i):
        s = ks((x, left, right, far)[kind], order[i], 1 - a)
        arrived(kv.at[s], sibr.at[kind, i], conds[kind])

    def image_line(dz):
        part = img.at[pl.ds(si(0, (z + 4 - dz) % 4, a), 3)]
        if dz > 0:
            arrived(part, izr.at[dz])
        send(part, part, isibs.at[dz], isibr.at[dz], ctx(x, z, 1 - a), h)

    def block_bias(i, b):
        qb = 2 * c + i
        shown = jnp.where(b < qb, mask[qb, b], 0)
        return jnp.full((1, BLK), jnp.where(shown == 1, 0.0, HIDDEN), F32)

    def fill(kind, half):
        for u in range(2):
            for w in range(2):
                x_ = (x, left, right, far)[kind]
                core = a if w == 0 else 1 - a
                z_ = order[2 * half + u]
                s = ks(x_, z_, core)
                t = 4 * u + 2 * w
                keys[t * BLK:(t + 2) * BLK, :] = kv[s, :256, :]
                vals[t * BLK:(t + 2) * BLK, :128] = kv[s, 256:, :]
                for n in range(2):
                    for i in range(2):
                        bias[i, :, (t + n) * BLK:(t + n + 1) * BLK] = block_bias(
                            i, 2 * ctx(x_, z_, core) + n
                        )

    def work(kind, half, part=None):
        def extra(i, r):
            if (kind, half) != (0, 0):
                return bias[i]
            at = lax.broadcasted_iota(jnp.int32, (TILE, BLK), 0) // GROUP + r * (TILE // GROUP)
            key = lax.broadcasted_iota(jnp.int32, (TILE, BLK), 1)
            tri = jnp.where(key <= at, 0.0, HIDDEN)
            full = jnp.broadcast_to(bias[i], (TILE, SPAN * BLK))
            parts = [full[:, :i * BLK], tri, full[:, (i + 1) * BLK:]]
            return jnp.concatenate(parts[1 - min(i, 1):], axis=1)

        def go():
            if part != 1:
                fill(kind, half)
            for i in range(2):
                if part is None or part == i:
                    soft_step(q, keys, vals, acc, top, i * ROWS, functools.partial(extra, i))

        run(((None, z > 1), (x > 0,) * 2, (x == 3,) * 2, (x > 1,) * 2)[kind][half], go)

    s = ks(x, z, a)
    along_x(0, 0)
    along_x(0, 1)
    for i in range(1, 4):
        send(own, kv.at[s], zs.at[i], zr.at[z], ctx(x, order[i], a), h)
    share(0, 0)

    vals[:, 128:] = jnp.ones((SPAN * BLK, 128), BF16)
    top[...] = jnp.full_like(top, FLOOR)
    acc[...] = jnp.zeros_like(acc)
    loads[4].wait()
    loads[5].wait()
    keep_own.wait()

    column(1)
    from_left(0)
    from_right(0)

    inbox[0] = outbox[h]
    for d in range(1, HEADS):
        arrived(inbox.at[d], piece_r.at[d])
    rows = inbox[...].astype(F32)
    si_mine = si(x, z, a)
    own_img[:64] = rows[:, :8, :].reshape(64, 128).astype(BF16)
    own_img[64:] = rows[:, 8:, :].reshape(64, 128).astype(BF16)
    keep_img = pltpu.make_async_copy(own_img, img.at[si_mine], keep.at[1])
    keep_img.start()
    for d, x_ in ((1, right), (2, far), (3, left)):
        send(own_img, img.at[si_mine], ixs.at[d], ixr.at[d], ctx(x_, z, a), h, x < 3)
    nth = jnp.minimum(jnp.maximum(c - 24, 0), 6)
    send(own_img, img.at[si_mine], last_s.at[0], last_r.at[nth], LAST, h, final)

    other_core(0, 0)
    other_core(0, 1)
    work(0, 0, 0)
    column(2)
    from_left(1)
    from_right(1)
    work(0, 0, 1)
    column(3)
    for d, x_ in ((1, left), (2, far), (3, right)):
        arrived(img.at[si(x_, z, a)], ixr.at[d], (x + 4 - d) % 4 < 3)
    keep_img.wait()
    part = img.at[pl.ds(si(0, z, a), 3)]
    for dz in (1, 3, 2):
        send(part, part, izs.at[dz], izr.at[dz], ctx(x, (z + dz) % 4, a), h)
    image_line(0)
    other_core(1, 0)
    other_core(1, 1)
    work(1, 0, 0)
    from_right(2)
    from_left(2)
    work(1, 0, 1)
    from_right(3)
    from_left(3)
    other_core(2, 0)
    other_core(2, 1)
    from_far(0)
    work(2, 0)
    from_far(1)
    image_line(1)
    other_core(0, 2)
    other_core(0, 3)
    image_line(3)
    from_far(2)
    work(0, 1)
    image_line(2)
    other_core(3, 0)
    other_core(3, 1)
    work(3, 0)
    from_far(3)
    for kind in (1, 2, 3):
        other_core(kind, 2)
        other_core(kind, 3)
        if (kind, 1) not in LATER:
            work(kind, 1)
    for i in range(4):
        part = img.at[pl.ds(si(0, (z + 4 - i) % 4, 1 - a), 3)]
        arrived(part, isibr.at[i])
    for n in range(7):
        block = img.at[si(3, n // 2, n % 2)]
        arrived(block, last_r.at[n], c == LAST)
    for when, done in pending:
        run(when, done)


def attend_kernel(
    offsets_hbm, first_hbm, mask_hbm, q_hbm, kv, img, acc, top, self_hbm, cross_hbm,
    q, keys, vals, acc2, top2, bias, out, seen, offsets, first, mask, sems,
):
    c = lax.axis_index("ctx")
    x, z = c // 8, (c // 2) % 4
    loads = [
        pltpu.make_async_copy(src, dst, sems.at[n])
        for n, (src, dst) in enumerate((
            (mask_hbm, mask), (offsets_hbm, offsets), (first_hbm, first), (q_hbm, q),
        ))
    ]
    for load in loads:
        load.start()
    vals[:, :, 128:] = jnp.ones((2, SPAN * BLK, 128), BF16)
    top2[...] = jnp.full_like(top2, FLOOR)
    acc2[...] = jnp.zeros_like(acc2)
    for load in loads:
        load.wait()

    def result(a_ref):
        total = a_ref[:, 128:]
        good = total > 0.0
        return jnp.where(good, a_ref[:, :128] / jnp.where(good, total, 1.0), 0.0).astype(BF16)

    def cross(i, pair):
        qb = 2 * c + i
        both = (2 * pair, 2 * pair + 1)
        lowest = [jnp.where(m >= first[qb], offsets[m], 1 << 30) for m in both]
        last = qb * BLK + BLK - 1

        @pl.when((lowest[0] <= last) | (lowest[1] <= last))
        def _():
            for n, m in enumerate(both):
                for d in range(8):
                    held = jnp.where(c == LAST, m, m - 1) if m == IMAGES - 1 else m
                    s = (d % 2) * 16 + (d // 2) * 4 + held
                    row = n * IMG_LEN + d * 64
                    keys[i, row:row + 64, :] = img[s, :64, :]
                    vals[i, row:row + 64, :128] = img[s, 64:, :]

            def extra(r):
                at = lax.broadcasted_iota(jnp.int32, (TILE, IMG_LEN), 0) // GROUP + (
                    r * (TILE // GROUP) + qb * BLK
                )
                return jnp.concatenate(
                    [jnp.where(at >= low, 0.0, HIDDEN) for low in lowest], axis=1
                )

            soft_step(q, keys.at[i], vals.at[i], acc2, top2, i * ROWS, extra)

    for pair in range(2):
        for i in range(2):
            cross(i, pair)
    out[1] = result(acc2)
    put_cross = pltpu.make_async_copy(out.at[1], cross_hbm, sems.at[4])
    put_cross.start()

    counts = []
    for i in range(2):
        qb = 2 * c + i
        n = jnp.int32(0)
        for kind, half in LATER:
            x_ = (x + 1) % 4 if kind == 2 else (x + 2) % 4
            there = (x == 3) if kind == 2 else (x > 1)
            for u in range(2):
                z_ = 2 - z // 2 if u == 0 else 3 - 3 * (z // 2)
                for w in range(4):
                    b = jnp.where(there, x_ * 16 + z_ * 4 + w, 0)
                    seen[i, n] = b
                    n = n + jnp.where(there, mask[qb, b], 0)
        counts.append(n)

    def span(j, _):
        for i in range(2):
            for t in range(SPAN):
                n = j * SPAN + t
                live = n < counts[i]
                b = jnp.where(live, seen[i, jnp.where(live, n, 0)], 2 * c)
                dev = b // 2
                s = (dev % 2) * 16 + (dev // 8) * 4 + (dev // 2) % 4
                half = pl.multiple_of((b % 2) * BLK, BLK)
                keys[i, t * BLK:(t + 1) * BLK, :] = kv[s, pl.ds(half, BLK), :]
                vals[i, t * BLK:(t + 1) * BLK, :128] = kv[s, pl.ds(256 + half, BLK), :]
                bias[i, :, t * BLK:(t + 1) * BLK] = jnp.full(
                    (1, BLK), jnp.where(live, 0.0, HIDDEN), F32
                )
        for i in range(2):
            soft_step(q, keys.at[i], vals.at[i], acc, top, i * ROWS, lambda r: bias[i])
        return 0

    steps = (jnp.maximum(counts[0], counts[1]) + SPAN - 1) // SPAN
    lax.fori_loop(0, steps, span, 0)
    out[0] = result(acc)
    put_self = pltpu.make_async_copy(out.at[0], self_hbm, sems.at[5])
    put_self.start()
    put_cross.wait()
    put_self.wait()


def attend_call(offsets, first, mask, q, kv, img, acc, top):
    vmem = pl.BlockSpec(memory_space=pltpu.VMEM)
    hbm = pl.BlockSpec(memory_space=pltpu.HBM)
    n = q.shape[0]
    return pl.pallas_call(
        attend_kernel,
        out_shape=(jax.ShapeDtypeStruct((n, 128), BF16),) * 2,
        in_specs=[hbm] * 4 + [vmem] * 4,
        out_specs=(hbm, hbm),
        scratch_shapes=[
            pltpu.VMEM((n, 128), BF16),
            pltpu.VMEM((2, SPAN * BLK, 128), BF16),
            pltpu.VMEM((2, SPAN * BLK, 256), BF16),
            pltpu.VMEM((n, 256), F32),
            pltpu.VMEM((n, 128), F32),
            pltpu.VMEM((2, 1, SPAN * BLK), F32),
            pltpu.VMEM((2, n, 128), BF16),
            pltpu.SMEM((2, 64), jnp.int32),
            pltpu.SMEM((IMAGES,), jnp.int32),
            pltpu.SMEM(first.shape, jnp.int32),
            pltpu.SMEM(mask.shape, jnp.int32),
            pltpu.SemaphoreType.DMA((6,)),
        ],
        compiler_params=pltpu.CompilerParams(vmem_limit_bytes=32 * 2**20),
    )(*[pltpu.with_memory_space_constraint(t, pltpu.HBM) for t in (offsets, first, mask, q)], kv, img, acc, top)


def gather_call(q, k, v, ik, iv, mask):
    vmem = pl.BlockSpec(memory_space=pltpu.VMEM)
    hbm = pl.BlockSpec(memory_space=pltpu.HBM)
    dma = pltpu.SemaphoreType.DMA
    n = q.shape[0] * q.shape[1]
    rows = q.reshape(n, 128)
    return pl.pallas_call(
        gather_kernel,
        out_shape=(
            jax.ShapeDtypeStruct((32, 512, 128), BF16),
            jax.ShapeDtypeStruct((32, 128, 128), BF16),
            jax.ShapeDtypeStruct((n, 256), F32),
            jax.ShapeDtypeStruct((n, 128), F32),
        ),
        in_specs=[hbm] * 6,
        out_specs=(vmem,) * 4,
        scratch_shapes=[
            pltpu.VMEM((512, 128), BF16),
            pltpu.VMEM((128, 128), BF16),
            pltpu.VMEM((8, 16, 128), BF16),
            pltpu.VMEM((8, 16, 128), BF16),
            pltpu.VMEM((8, 8, 128), BF16),
            pltpu.VMEM((8, 8, 128), BF16),
            pltpu.VMEM((n, 128), BF16),
            pltpu.SMEM(mask.shape, jnp.int32),
            pltpu.VMEM((SPAN * BLK, 128), BF16),
            pltpu.VMEM((SPAN * BLK, 256), BF16),
            pltpu.VMEM((2, 1, SPAN * BLK), F32),
            dma((8,)), dma((8,)),
            dma((4,)), dma((4,)),
            dma((2, 2, 4)), dma((2, 2, 4)),
            dma((2, 4)), dma((2, 4)),
            dma((4, 4)), dma((4, 4)),
            dma((4,)), dma((4,)),
            dma((4,)), dma((4,)),
            dma((4,)), dma((4,)),
            dma((1,)), dma((7,)),
            dma((8,)),
        ],
        compiler_params=pltpu.CompilerParams(
            collective_id=0, has_side_effects=True, vmem_limit_bytes=32 * 2**20
        ),
    )(*[pltpu.with_memory_space_constraint(t, pltpu.HBM) for t in (k.reshape(-1, 128), v.reshape(-1, 128), ik, iv, rows, mask)])


def per_device(q, k, v, ik, iv, offsets, first, mask):
    kv, img, acc, top = gather_call(q, k, v, ik, iv, mask)
    rows = q.reshape(-1, 128)
    self_out, cross_out = attend_call(offsets, first, mask, rows, kv, img, acc, top)
    return self_out.reshape(q.shape), cross_out.reshape(q.shape)


def solution(mesh):
    return jax.shard_map(
        per_device,
        mesh=mesh,
        in_specs=(
            P("ctx", "head", None),
            P("ctx", "head", None),
            P("ctx", "head", None),
            P(("ctx", "head"), None, None),
            P(("ctx", "head"), None, None),
            P(),
            P(),
            P(),
        ),
        out_specs=(P("ctx", "head", None), P("ctx", "head", None)),
        check_vma=False,
    )
```

time: 71.7 us -> 59.5 us (0.83)
  local copies, waits for them, and re-layouts: 6.21 us -> 0 us
  Pallas kernels: 64.4 us -> 58.5 us
    unnamed x16 -> x0, local copies, waits for them, and re-layouts: 6.21 us -> none
    pallas_call x2, Pallas kernels: 64.4 us -> 58.5 us  [the longest x1 45.2 us: gather_call(): pl.pallas_call(gather_kernel, out_shape=(jax.ShapeDtypeStruct((32, 512, 1...]
where the time goes in v2:
time: 59.5 us; the launch traced here: 59.3 us
  Pallas kernels  58.5 us (98%)
  between operations  0.82 us (1%)
    pallas_call x1, Pallas kernels, gather_call(): pl.pallas_call(gather_kernel, out_shape=(jax.ShapeDtypeStruct((32, 512, 1...  45.2 us
    pallas_call x1, Pallas kernels, attend_call(): pl.pallas_call(attend_kernel, out_shape=(jax.ShapeDtypeStruct((n, 128), B...  13.3 us

profile of v2, /device:TPU:7, one launch (start us, length us, event | category | flops | bytes accessed | tf_op | source)
XLA Modules:
  0.0 59.3 jit_solution(17735509937430832377)
XLA Ops:
  0.6 45.2 %shard_map.95 = (bf16[32,512,128]{2,1,0:T(8,128)(2,1)S(1)}, bf16[32,128,128]{2,1,0:T(8,128)(2,1)S(1)}, f32[2048,256]{1,0:T(8,128)S(1)}, f32[2048,128]{1,0:T(8,128)S(1)}) custom-call(bf16[256,128]{1,0:T(8,128)(2,1)} %bitcast.7, bf16[256,128]{1,0:T(8,128)(2,1)} %bitcast.8, bf16[8,8,128]{2,1,0:T(8,128)(2,1)} %ik_hbm.1, bf16[8,8,128]{2,1,0:T(8,128)(2,1)} %iv_hbm.1, ...), custom_call_target="tpu_custom_call" | custom-call | tf_op jit(solution)/shard_map/pallas_call | solution.py:451
  45.8 13.3 %shard_map.96 = (bf16[2048,128]{1,0:T(8,128)(2,1)}, bf16[2048,128]{1,0:T(8,128)(2,1)}) custom-call(s32[4]{0:T(128)} %offsets_hbm.1, s32[64]{0:T(128)} %first_hbm.1, s32[64,64]{1,0:T(8,128)} %mask_hbm.3, bf16[2048,128]{1,0:T(8,128)(2,1)} %bitcast.6, bf16[32,512,128]{2,1,0:T(8,128)(2,1)S(1)} %get-tuple-element.8.kv, ...), custom_call_target="tpu_custom_call" | custom-call | tf_op jit(solution)/shard_map/pallas_call | solution.py:422
